TPU v7x, 512 devices: a whole 4x8x8 slice. The times are simulated.
512 devices in a mesh: dp: 16 (over y, core), proto: 32 (over z, x).
Axes of the slice: x: 4, y: 8, z: 8, core: 2. Of those that a mesh axis runs over, the one named last changes fastest.
Arguments:
- teacher_feat: bfloat16 [6144, 384], P('dp'), may hold values from -3 to 3
- student_feat: bfloat16 [6144, 384], P('dp'), may hold values from -3 to 3
- prototypes: bfloat16 [131072, 384], P('proto'), may hold values from -3 to 3
- row_weight: float32 [6144], P('dp'), may hold values from 200 to 2000
Outputs:
- row_loss: float32 [6144], P('dp')
- grad_student: float32 [6144, 384], P(('dp', 'proto'))
- grad_proto: bfloat16 [131072, 384], P(('proto', 'dp'))
All inputs are finite; a program needn't handle non-finite values.
Results may differ from a plain program's by a relative error of at most 0.03.
Values may be sent and summed in bfloat16 or wider, within the bound.
A program may use at most 64 MiB of HBM per device.

v0:
```python
import jax
import jax.numpy as jnp
from jax import lax
from jax.sharding import PartitionSpec as P

ITERS = 3


teacher_temp = 0.04
student_temp = 0.1
norm_eps = 1e-06


def normalize_rows(values):
    floats = values.astype(jnp.float32)
    length = jnp.sqrt(jnp.sum(floats * floats, axis=-1, keepdims=True) + norm_eps)
    return (floats / length, length)


def project(values, unit, length):
    return (values - unit * jnp.sum(unit * values, axis=-1, keepdims=True)) / length


def column_step(expo, rowscale):
    totals = lax.psum(jnp.sum(expo * rowscale[:, None], axis=0), "dp")
    return 1.0 / totals


def row_step(weighted):
    return 1.0 / lax.psum(jnp.sum(weighted, axis=1), "proto")


def shards(teacher_feat, student_feat, prototypes, row_weight):
    wunit, wnorm = normalize_rows(prototypes)
    wn = wunit.astype(jnp.bfloat16)
    tunit, tlength = normalize_rows(teacher_feat)
    tn = tunit.astype(jnp.bfloat16)
    sunit, snorm = normalize_rows(student_feat)
    sn = sunit.astype(jnp.bfloat16)
    contract = (((1,), (1,)), ((), ()))
    expo = jnp.exp(
        lax.dot_general(tn, wn, contract, preferred_element_type=jnp.float32) / teacher_temp
    )
    scores = lax.dot_general(sn, wn, contract, preferred_element_type=jnp.float32) / student_temp
    expsum_local = jnp.sum(jnp.exp(scores), axis=1)
    rowscale = jnp.ones((expo.shape[0],), jnp.float32)
    for step in range(ITERS):
        colscale = column_step(expo, rowscale)
        rowscale = row_step(expo * colscale[None, :])
    qz_local = jnp.sum(expo * colscale[None, :] * scores, axis=1)
    expsum, qz_pre = lax.psum((expsum_local, qz_local), "proto")
    lse = jnp.log(expsum)
    row_loss = lse - rowscale * qz_pre
    probs = jnp.exp(scores - lse[:, None])
    target = expo * colscale[None, :] * rowscale[:, None]
    dscore = (row_weight[:, None] * (probs - target) / student_temp).astype(jnp.bfloat16)
    xg = lax.dot_general(dscore, sn, (((0,), (0,)), ((), ())), preferred_element_type=jnp.float32)
    grad_proto = lax.psum_scatter(
        project(xg, wunit, wnorm).astype(jnp.bfloat16), "dp", scatter_dimension=0, tiled=True
    )
    my_rows = dscore.shape[0] // lax.axis_size("proto")
    dsn = lax.psum_scatter(
        jnp.dot(dscore, wn, preferred_element_type=jnp.float32).astype(jnp.bfloat16),
        "proto",
        scatter_dimension=0,
        tiled=True,
    ).astype(jnp.float32)
    offset = lax.axis_index("proto") * my_rows
    unit_rows = lax.dynamic_slice_in_dim(sunit, offset, my_rows, 0)
    norm_rows = lax.dynamic_slice_in_dim(snorm, offset, my_rows, 0)
    grad_student = project(dsn, unit_rows, norm_rows)
    return (row_loss, grad_student, grad_proto)


def solution(mesh):
    return jax.shard_map(
        shards,
        mesh=mesh,
        in_specs=(P("dp", None), P("dp", None), P("proto", None), P("dp")),
        out_specs=(P("dp"), P(("dp", "proto"), None), P(("proto", "dp"), None)),
        check_vma=False,
    )
```

profile of v0, /device:TPU:70, one launch (start us, length us, event | category | flops | bytes accessed | tf_op | source)
XLA Modules:
  0.0 526.5 jit_solution(14824692578550391598)
XLA Ops:
  7.2 0.0 reduce-scatter.4.cloned.1.call-start
  7.2 3.2 copy.9
  10.4 0.7 fusion.1
  11.2 0.1 fusion.4
  11.3 4.5 fusion.17
  15.9 48.5 %psum.57 = f32[4096]{0:T(1024)S(1)} all-reduce(f32[4096]{0:T(1024)S(1)} %get-tuple-element.18), channel_id=1, replica_groups=mesh['dp'=16,'proto'=32] {'dp'}, use_global_device_ids=true, to_apply=%region_6.0 | all-reduce | flops 4096 | bytes 32768 | tf_op jit(solution)/shard_map/psum | solution.py:25
  64.3 3.3 multiply_reduce_fusion.5
  67.6 65.9 %psum.58 = f32[384]{0:T(512)S(1)} all-reduce(f32[384]{0:T(512)S(1)} %multiply_reduce_fusion.5), channel_id=1, replica_groups=mesh['dp'=16,'proto'=32] {'proto'}, use_global_device_ids=true, to_apply=%region_8.0 | all-reduce | flops 384 | bytes 3072 | tf_op jit(solution)/shard_map/psum | solution.py:30
  133.6 3.6 multiply_reduce_fusion.4
  137.2 45.7 %psum.59 = f32[4096]{0:T(1024)S(1)} all-reduce(f32[4096]{0:T(1024)S(1)} %multiply_reduce_fusion.4), channel_id=1, replica_groups=mesh['dp'=16,'proto'=32] {'dp'}, use_global_device_ids=true, to_apply=%region_10.0 | all-reduce | flops 4096 | bytes 32768 | tf_op jit(solution)/shard_map/psum | solution.py:25
  182.9 3.4 multiply_reduce_fusion.3
  186.3 74.1 %psum.60 = f32[384]{0:T(512)S(1)} all-reduce(f32[384]{0:T(512)S(1)} %multiply_reduce_fusion.3), channel_id=1, replica_groups=mesh['dp'=16,'proto'=32] {'proto'}, use_global_device_ids=true, to_apply=%region_12.0 | all-reduce | flops 384 | bytes 3072 | tf_op jit(solution)/shard_map/psum | solution.py:30
  260.4 3.6 multiply_reduce_fusion.2
  264.1 45.7 %psum.61 = f32[4096]{0:T(1024)S(1)} all-reduce(f32[4096]{0:T(1024)S(1)} %multiply_reduce_fusion.2), channel_id=1, replica_groups=mesh['dp'=16,'proto'=32] {'dp'}, use_global_device_ids=true, to_apply=%region_14.0 | all-reduce | flops 4096 | bytes 32768 | tf_op jit(solution)/shard_map/psum | solution.py:25
  309.8 0.1 fusion.3
  309.9 0.0 copy-start.3
  310.0 6.6 %multiply_reduce_fusion.6 = (f32[384]{0:T(512)S(1)}, f32[384]{0:T(512)S(1)}, f32[384]{0:T(512)S(1)}, f32[384,4096]{1,0:T(8,128)}) fusion(f32[384,4096]{1,0:T(8,128)} %get-tuple-element.19, f32[4096]{0:T(1024)S(1)} %broadcast_divide_fusion, f32[4096]{0:T(1024)S(1)} %add_sqrt_fusion, bf16[4096,384]{0,1:T(8,128)(2,1)S(1)} %copy.9, f32[384]{0:T(512)S(1)} %add_sqrt_fusion.2, ...), kind=kOutput, calls=%fused_computation.14 | convolution fusion | flops 1222556544 | bytes 16062464 | tf_op jit(solution)/shard_map/dot_general | solution.py:44
  316.5 70.8 %all-reduce.2 = (f32[384]{0:T(512)S(1)}, f32[384]{0:T(512)S(1)}, f32[384]{0:T(512)S(1)}) all-reduce(f32[384]{0:T(512)S(1)} %get-tuple-element.10, f32[384]{0:T(512)S(1)} %get-tuple-element.11, f32[384]{0:T(512)S(1)} %get-tuple-element.9), channel_id=1, replica_groups=mesh['dp'=16,'proto'=32] {'proto'}, use_global_device_ids=true, to_apply=%region_18.0 | all-reduce | flops 1152 | bytes 9216 | tf_op jit(solution)/shard_map/psum | solution.py:51
  387.3 0.6 fusion.16
  387.9 5.8 %multiply_convert_fusion = bf16[384,4096]{1,0:T(8,128)(2,1)S(1)} fusion(f32[384,4096]{1,0:T(8,128)} %get-tuple-element.20, f32[384,4096]{1,0:T(8,128)} %get-tuple-element.19, f32[384]{0:T(512)S(1)} %get-tuple-element.17, f32[384]{0:T(512)S(1)} %get-tuple-element.15, f32[384]{0:T(512)S(1)} %copy-done.3, f32[4096]{0:T(1024)S(1)} %broadcast_divide_fusion), kind=kLoop, calls=%fused_computation.5 | loop fusion | flops 11010048 | bytes 15749632 | tf_op jit(solution)/shard_map/convert_element_type | solution.py:56
  393.7 2.2 multiply_reduce_fusion
  395.9 2.5 divide_convert_fusion
  398.4 0.0 reduce-scatter.4.cloned.1.call-update
  398.5 4.4 convolution_convert_fusion
  402.9 73.9 %fusion = bf16[16,384]{1,0:T(8,128)(2,1)S(1)} fusion(bf16[384,384]{1,0:T(8,128)(2,1)} %convolution_convert_fusion), kind=kCustom, calls=%all-reduce-scatter | all-reduce-scatter fusion | flops 196609 | bytes 309248
  476.8 1.9 collective-permute-start
  478.7 2.5 collective-permute-start.1
  481.3 11.7 %collective-permute-start.7 = (bf16[12,384]{1,0:T(8,128)(2,1)S(1)}, bf16[12,384]{1,0:T(8,128)(2,1)S(1)}, u32[]{:S(2)}, u32[]{:S(2)}) collective-permute-start(bf16[12,384]{1,0:T(8,128)(2,1)S(1)} %slice), channel_id=1, source_target_pairs={{0,8},{1,9},{2,10},{3,11},{4,12},{5,13},{6,14},{7,15},{8,16},{9,17... | collective-permute-start | bytes 27656
  493.0 1.9 collective-permute-start.2
  494.9 3.3 collective-permute-start.3
  498.2 0.0 collective-permute-done.7
  498.2 6.8 %collective-permute-start.4 = (bf16[16,384]{1,0:T(8,128)(2,1)S(1)}, bf16[16,384]{1,0:T(8,128)(2,1)S(1)}, u32[]{:S(2)}, u32[]{:S(2)}) collective-permute-start(bf16[16,384]{1,0:T(8,128)(2,1)S(1)} %fusion), channel_id=1, source_target_pairs={{0,5},{1,6},{2,7},{3,8},{4,9},{5,10},{6,11},{7,12},{8,13},{9,14},{... | collective-permute-start | bytes 36872
  505.1 0.0 collective-permute-done
  505.1 3.0 collective-permute-start.5
  508.1 0.0 collective-permute-done.1
  508.1 1.9 collective-permute-start.6
  510.0 0.1 convert_divide_fusion.2
  510.2 0.1 dynamic-slice.3
  510.3 1.3 dynamic-slice.8
  512.2 0.0 collective-permute-done.2
  512.2 0.0 collective-permute-done.3
  512.2 0.0 collective-permute-done.4
  512.2 0.8 collective-permute-done.5
  513.1 2.8 collective-permute-done.6
  515.8 1.2 concatenate
  517.0 0.1 fusion.11
  517.2 0.7 fusion.12
  517.9 1.7 copy.10
  (17 shorter events, 0.1 us)
Async XLA Ops:
  7.2 4.0 copy-start.2
  7.2 510.7 %reduce-scatter.4.cloned.1.call-start = ((), (), s32[]{:S(2)}) async-start(), calls=%async_computation.1 | async-start | bytes 3342336 | tf_op jit(solution)/shard_map/reduce_scatter | solution.py:58
  182.9 126.9 %copy-start.1 = (bf16[384,384]{1,0:T(8,128)(2,1)S(1)}, bf16[384,384]{1,0:T(8,128)(2,1)}, u32[]{:S(2)}) copy-start(bf16[384,384]{1,0:T(8,128)(2,1)} %param.5) | copy-start | bytes 884740
  309.9 78.0 %copy-start.3 = (f32[384]{0:T(512)S(1)}, f32[384]{0:T(512)}, u32[]{:S(2)}) copy-start(f32[384]{0:T(512)} %param.7) | copy-start | bytes 4612
  393.7 2.2 copy-start
  476.8 28.3 %collective-permute-start = (bf16[16,384]{1,0:T(8,128)(2,1)S(1)}, bf16[16,384]{1,0:T(8,128)(2,1)S(1)}, u32[]{:S(2)}, u32[]{:S(2)}) collective-permute-start(bf16[16,384]{1,0:T(8,128)(2,1)S(1)} %fusion), channel_id=1, source_target_pairs={{0,1},{1,2},{2,3},{3,4},{4,5},{5,6},{6,7},{7,8},{8,9},{9,10},{10,1... | collective-permute-start | bytes 36872
  478.7 29.4 %collective-permute-start.1 = (bf16[16,384]{1,0:T(8,128)(2,1)S(1)}, bf16[16,384]{1,0:T(8,128)(2,1)S(1)}, u32[]{:S(2)}, u32[]{:S(2)}) collective-permute-start(bf16[16,384]{1,0:T(8,128)(2,1)S(1)} %fusion), channel_id=1, source_target_pairs={{0,2},{1,3},{2,4},{3,5},{4,6},{5,7},{6,8},{7,9},{8,10},{9,11},{10,... | collective-permute-start | bytes 36872
  481.3 17.0 %collective-permute-start.7 = (bf16[12,384]{1,0:T(8,128)(2,1)S(1)}, bf16[12,384]{1,0:T(8,128)(2,1)S(1)}, u32[]{:S(2)}, u32[]{:S(2)}) collective-permute-start(bf16[12,384]{1,0:T(8,128)(2,1)S(1)} %slice), channel_id=1, source_target_pairs={{0,8},{1,9},{2,10},{3,11},{4,12},{5,13},{6,14},{7,15},{8,16},{9,17... | collective-permute-start | bytes 27656
  493.0 19.2 %collective-permute-start.2 = (bf16[16,384]{1,0:T(8,128)(2,1)S(1)}, bf16[16,384]{1,0:T(8,128)(2,1)S(1)}, u32[]{:S(2)}, u32[]{:S(2)}) collective-permute-start(bf16[16,384]{1,0:T(8,128)(2,1)S(1)} %fusion), channel_id=1, source_target_pairs={{0,3},{1,4},{2,5},{3,6},{4,7},{5,8},{6,9},{7,10},{8,11},{9,12},{10... | collective-permute-start | bytes 36872
  494.9 17.3 %collective-permute-start.3 = (bf16[16,384]{1,0:T(8,128)(2,1)S(1)}, bf16[16,384]{1,0:T(8,128)(2,1)S(1)}, u32[]{:S(2)}, u32[]{:S(2)}) collective-permute-start(bf16[16,384]{1,0:T(8,128)(2,1)S(1)} %fusion), channel_id=1, source_target_pairs={{0,4},{1,5},{2,6},{3,7},{4,8},{5,9},{6,10},{7,11},{8,12},{9,13},{1... | collective-permute-start | bytes 36872
  498.2 14.0 %collective-permute-start.4 = (bf16[16,384]{1,0:T(8,128)(2,1)S(1)}, bf16[16,384]{1,0:T(8,128)(2,1)S(1)}, u32[]{:S(2)}, u32[]{:S(2)}) collective-permute-start(bf16[16,384]{1,0:T(8,128)(2,1)S(1)} %fusion), channel_id=1, source_target_pairs={{0,5},{1,6},{2,7},{3,8},{4,9},{5,10},{6,11},{7,12},{8,13},{9,14},{... | collective-permute-start | bytes 36872
  505.1 8.0 %collective-permute-start.5 = (bf16[16,384]{1,0:T(8,128)(2,1)S(1)}, bf16[16,384]{1,0:T(8,128)(2,1)S(1)}, u32[]{:S(2)}, u32[]{:S(2)}) collective-permute-start(bf16[16,384]{1,0:T(8,128)(2,1)S(1)} %fusion), channel_id=1, source_target_pairs={{0,6},{1,7},{2,8},{3,9},{4,10},{5,11},{6,12},{7,13},{8,14},{9,15},... | collective-permute-start | bytes 36872
  508.1 7.7 %collective-permute-start.6 = (bf16[16,384]{1,0:T(8,128)(2,1)S(1)}, bf16[16,384]{1,0:T(8,128)(2,1)S(1)}, u32[]{:S(2)}, u32[]{:S(2)}) collective-permute-start(bf16[16,384]{1,0:T(8,128)(2,1)S(1)} %fusion), channel_id=1, source_target_pairs={{0,7},{1,8},{2,9},{3,10},{4,11},{5,12},{6,13},{7,14},{8,15},{9,16}... | collective-permute-start | bytes 36872
Sparse Core Ops, SparseCore 0:
  398.6 66.4 reduce-scatter.3
where the time goes:
time: 527 us; the launch traced here: 526 us
  blocking collectives  425 us (81%)
  starting transfers between devices  33.2 us (6%)
  other arithmetic  24.8 us (5%)
  matrix products  17.7 us (3%)
  between operations  14.9 us (3%)
  local copies, waits for them, and re-layouts  7.54 us (1%)
    psum x2, blocking collectives, row_step(): return 1.0 / lax.psum(jnp.sum(weighted, axis=1), 'proto')  140 us
    psum x3, blocking collectives, column_step(): totals = lax.psum(jnp.sum(expo * rowscale[:, None], axis=0), 'dp')  140 us
    unnamed x1, blocking collectives  73.9 us
    psum x1, blocking collectives, shards(): expsum, qz_pre = lax.psum((expsum_local, qz_local), 'proto')  70.8 us
    unnamed x8, starting transfers between devices  33.2 us
  transfers between devices with their start and end apart: 9, of which 2 were waited for; matrix products, arithmetic and copies ran while one was open for 16% of the time, Pallas kernels for 0%

commit v1 on v0

v1 whole, which is shorter than its diff:
```python
import jax
import jax.numpy as jnp
from jax import lax
from jax.experimental import pallas as pl
from jax.experimental.pallas import tpu as pltpu
from jax.sharding import PartitionSpec as P

MESH = pl.DeviceIdType.MESH
F32, BF16 = jnp.float32, jnp.bfloat16
ITERS = 3
NY, NC, NZ, NX = 8, 2, 8, 4
NP = NZ * NX
R = 384
D = 384
KB = 256
NB = 8
ZR = R // NZ
PR = R // NP
EPS = 1e-6
NT = (((1,), (1,)), ((), ()))


def hops(step, size):
    return min(step, size - step)


Y_STEPS = sorted(range(1, NY), key=lambda a: -hops(a, NY))
Z_STEPS = sorted(range(1, NZ), key=lambda a: -hops(a, NZ))
X_STEPS = sorted(range(1, NX), key=lambda a: -hops(a, NX))
ZX_STEPS = sorted(
    [(a, b) for a in range(NZ) for b in range(NX) if (a, b) != (0, 0)],
    key=lambda s: -(hops(s[0], NZ) + hops(s[1], NX)),
)


def unit_rows(values):
    floats = values.astype(F32)
    return floats * lax.rsqrt(jnp.sum(floats * floats, axis=-1, keepdims=True) + EPS)


def two_rows(vector):
    high = vector.astype(BF16).astype(F32)
    low = vector - high
    rows = lax.broadcasted_iota(jnp.int32, (16, vector.shape[1]), 0)
    return jnp.where(rows == 0, high, jnp.where(rows == 1, low, 0.0)).astype(BF16)


def pack(vectors, rows):
    parts = [v[:, j : j + 128] for v in vectors for j in range(0, v.shape[1], 128)]
    if len(parts) < rows:
        parts.append(jnp.zeros((rows - len(parts), 128), F32))
    return jnp.concatenate(parts, axis=0)


def unpack(tile, start, count):
    return jnp.concatenate([tile[j : j + 1, :] for j in range(start, start + count)], axis=1)


def kernel(
    t_ref, s_ref, w_ref, rw_ref, loss_ref, gs_ref, gp_ref,
    wraw, wfraw, wn, wnt, wnf, tn2, sn2, gt, gs, snt, expo, expoz, prob, ef, pf, uw,
    vacc, scaled, cvec, ybuf, zxbuf, cbuf, c3buf, auxc, auxzx, abuf, bbuf,
    ucs, ucr, uzs, uzr, uxs, uxr, vsend, vrecv, bsend, brecv,
    wsem, xs, xr, ys, yr, zxs, zxr, cs, cr, gts, gtr, tcs, tcr, scs, scr, abs_, abr,
    us, ur, vbs, vbr,
):
    dp, pr = lax.axis_index("dp"), lax.axis_index("proto")
    y, c = lax.div(dp, NC), lax.rem(dp, NC)
    z, x = lax.div(pr, NX), lax.rem(pr, NX)
    o = 1 - c

    def dev(yy, cc, zz, xx):
        return {"dp": yy * NC + cc, "proto": zz * NX + xx}

    sibling = dev(y, o, z, x)
    y_at = lambda a: lax.rem(y + a, NY)
    z_at = lambda a: lax.rem(z + a, NZ)
    x_at = lambda a: lax.rem(x + a, NX)
    late = []

    def wait_for(ref, sem):
        pltpu.make_async_copy(ref, ref, sem).wait()

    def send(src, dst, ss, rs, to):
        pltpu.make_async_remote_copy(
            src_ref=src, dst_ref=dst, send_sem=ss, recv_sem=rs, device_id=to, device_id_type=MESH
        ).start()

    def send_y(ref, ss, rs):
        for a in Y_STEPS:
            send(ref.at[y], ref.at[y], ss, rs, dev(y_at(a), c, z, x))
        late.append((ref.at[pl.ds(0, NY - 1)], ss))

    def send_zx(ref, ss, rs):
        for a, b in ZX_STEPS:
            send(ref.at[pr], ref.at[pr], ss, rs, dev(y, c, z_at(a), x_at(b)))
        late.append((ref.at[pl.ds(0, NP - 1)], ss))

    def send_core(src, dst, ss, rs):
        send(src, dst, ss, rs, sibling)
        late.append((src, ss))

    loads = [
        pltpu.make_async_copy(w_ref.at[pl.ds((2 * b + c) * KB, KB)], wraw.at[b], wsem.at[b])
        for b in range(NB)
    ]
    loads.append(pltpu.make_async_copy(w_ref.at[pl.ds(2 * y * KB, 2 * KB)], wfraw, wsem.at[NB]))
    for load in loads:
        load.start()
    barrier = pltpu.get_barrier_semaphore()
    peers = [sibling]
    peers += [dev(y, c, z_at(a), x_at(b)) for a, b in ZX_STEPS]
    peers += [dev(y_at(a), c, z, x) for a in Y_STEPS]
    for peer in peers:
        pl.semaphore_signal(barrier, inc=1, device_id=peer, device_id_type=MESH)

    tn2[c] = unit_rows(t_ref[...]).astype(BF16)
    sn_own = unit_rows(s_ref[...]).astype(BF16)
    sn2[c] = sn_own
    gs[y] = sn_own
    gt[z, y] = tn2[c, pl.ds(pl.multiple_of(z * ZR, 16), ZR), :]
    for load in loads:
        load.wait()

    def norm_block(b, carry):
        block = unit_rows(wraw[b]).astype(BF16)
        wn[b] = block
        wnt[b] = block.T
        return carry

    lax.fori_loop(0, NB, norm_block, 0)
    for h in range(NC):
        wnf[h] = unit_rows(wfraw[pl.ds(h * KB, KB), :]).astype(BF16)

    def score_rows(h, first):
        def block(b, carry):
            w = wn[b]
            st = lax.dot_general(tn2[h], w, NT, preferred_element_type=F32)
            e = jnp.exp(st * 25.0)
            zs = lax.dot_general(sn2[h], w, NT, preferred_element_type=F32) * 10.0
            expo[b, h] = e.astype(BF16)
            expoz[b, h] = (e * zs).astype(BF16)
            prob[b, h] = jnp.exp(zs).astype(BF16)
            total = jnp.sum(e, axis=0, keepdims=True)
            if not first:
                total = total + ybuf[0, y, pl.ds(b, 1), :]
            ybuf[0, y, pl.ds(b, 1), :] = total
            return carry

        lax.fori_loop(0, NB, block, 0)

    score_rows(c, True)

    pl.semaphore_wait(barrier, len(peers))
    send_core(tn2.at[c], tn2.at[c], xs.at[0], xr.at[0])
    send_core(sn2.at[c], sn2.at[c], xs.at[1], xr.at[1])
    for a in Y_STEPS:
        send(gt.at[z, y], gt.at[z, y], gts.at[0], gtr.at[0], dev(y_at(a), c, z, x))
    late.append((gt.at[0, pl.ds(0, NY - 1)], gts.at[0]))

    def y_chain(step):
        if step > 1:
            for way, back in ((0, -(step - 1)), (1, step - 1)):
                wait_for(gs.at[y_at(NY + back)], scr.at[way, step - 2])
        for way, back, to in ((0, -(step - 1), 1), (1, step - 1, -1)):
            src = gs.at[y_at(NY + back)]
            if step == 4:
                src = src.at[pl.ds(way * (R // 2), R // 2)]
            send(src, src, scs.at[way, step - 1], scr.at[way, step - 1], dev(y_at(NY + to), c, z, x))
            late.append((src, scs.at[way, step - 1]))

    def y_chain_end():
        for way in range(2):
            wait_for(gs.at[y_at(4), pl.ds(way * (R // 2), R // 2)], scr.at[way, 3])

    def z_chain(step):
        if step == 1:
            wait_for(gt.at[z, pl.ds(0, NY - 1)], gtr.at[0])
        else:
            for way, back in ((0, -(step - 1)), (1, step - 1)):
                wait_for(gt.at[z_at(NZ + back)], tcr.at[way, step - 2])
        for way, back, to in ((0, -(step - 1), 1), (1, step - 1, -1)):
            src = gt.at[z_at(NZ + back)]
            if step == 4:
                src = src.at[pl.ds(way * (NY // 2), NY // 2)]
            send(src, src, tcs.at[way, step - 1], tcr.at[way, step - 1], dev(y, c, z_at(NZ + to), x))
            late.append((src, tcs.at[way, step - 1]))

    def z_chain_end():
        for way in range(2):
            wait_for(gt.at[z_at(4), pl.ds(way * (NY // 2), NY // 2)], tcr.at[way, 3])

    def fill_teacher(slice_):
        rows = gt[slice_].reshape(R, D)
        for h in range(NC):
            st = lax.dot_general(rows, wnf[h], NT, preferred_element_type=F32)
            e = jnp.exp(st * 25.0).astype(BF16)
            for g in range(NY):
                ef[h, g, slice_] = e[g * ZR : (g + 1) * ZR]

    def fill_student(group):
        rows = gs[group]
        snt[group] = rows.T
        for h in range(NC):
            zs = lax.dot_general(rows, wnf[h], NT, preferred_element_type=F32) * 10.0
            pf[group, h] = jnp.exp(zs).astype(BF16)

    y_chain(1)
    fill_student(y)
    wait_for(tn2.at[o], xr.at[0])
    wait_for(sn2.at[o], xr.at[1])
    score_rows(o, False)

    def own(v):
        return jnp.where(c == 0, v[:, :R], v[:, R:])

    def other(v):
        return jnp.where(c == 0, v[:, R:], v[:, :R])

    def row_sums(lhs, mats):
        sums = [jnp.zeros((16, NC * R), F32) for _ in mats]
        for b in range(NB):
            left = lhs(b)
            for i, mat in enumerate(mats):
                sums[i] = sums[i] + lax.dot_general(
                    left, mat[b].reshape(NC * R, KB), NT, preferred_element_type=F32
                )
        return [s[0:1] + s[1:2] for s in sums]

    def sum_protos(q, mat, scale):
        def half(h, carry):
            left = jnp.concatenate([mat[b, h] for b in range(NB)], axis=1)
            if scale is None:
                right = jnp.concatenate([wnt[b] for b in range(NB)], axis=1)
            else:
                right = jnp.concatenate(
                    [(wnt[b].astype(F32) * scale[b : b + 1, :]).astype(BF16) for b in range(NB)], axis=1
                )
            uw[q, h] = lax.dot_general(left, right, NT, preferred_element_type=F32)
            return carry

        lax.fori_loop(0, NC, half, 0)
        ucs[q] = uw[q, o].astype(BF16)
        send_core(ucs.at[q], ucr.at[q], us.at[q, 0], ur.at[q, 0])

    def student_z(q):
        wait_for(ucr.at[q], ur.at[q, 0])
        total = uw[q, c] + ucr[q].astype(F32)
        uzs[q] = total.astype(BF16).reshape(NZ, ZR, D)
        uzr[q, z] = uzs[q, z]
        for a in Z_STEPS:
            send(uzs.at[q, z_at(a)], uzr.at[q, z], us.at[q, 1], ur.at[q, 1], dev(y, c, z_at(a), x))
        late.append((uzs.at[q, pl.ds(0, NZ - 1)], us.at[q, 1]))

    def student_x(q):
        wait_for(uzr.at[q, pl.ds(0, NZ - 1)], ur.at[q, 1])
        total = jnp.sum(uzr[q].astype(F32), axis=0)
        pad = jnp.zeros((16 - PR, D), F32)
        for i in range(NX):
            uxs[q, i] = jnp.concatenate([total[i * PR : (i + 1) * PR], pad], axis=0).astype(BF16)
        uxr[q, x] = uxs[q, x]
        for a in X_STEPS:
            send(uxs.at[q, x_at(a)], uxr.at[q, x], us.at[q, 2], ur.at[q, 2], dev(y, c, z, x_at(a)))
        late.append((uxs.at[q, pl.ds(0, NX - 1)], us.at[q, 2]))

    def student_end(q):
        wait_for(uxr.at[q, pl.ds(0, NX - 1)], ur.at[q, 2])
        return jnp.sum(uxr[q].astype(F32), axis=0)

    rowscale = None
    for it in range(ITERS):
        last = it == ITERS - 1
        if it > 0:
            left = two_rows(rowscale)
            for b in range(NB):
                both = jnp.dot(left, expo[b].reshape(NC * R, KB), preferred_element_type=F32)
                ybuf[it, y, b : b + 1, :] = both[0:1] + both[1:2]
        send_y(ybuf.at[it], ys.at[it], yr.at[it])
        if it == 0:
            rows16 = lax.broadcasted_iota(jnp.int32, (16, KB), 0)
            ones = jnp.where(rows16 == 0, 1.0, 0.0).astype(BF16)
            (expsum,) = row_sums(lambda b: ones, [prob])
            auxc[0] = pack([other(expsum)], 4)
            send_core(auxc.at[0], auxc.at[1], cs.at[ITERS], cr.at[ITERS])
            expsum_own = own(expsum)
            sum_protos(0, prob, None)
        elif it == 1:
            wait_for(auxc.at[1], cr.at[ITERS])
            auxzx[pr] = pack([expsum_own], 4) + auxc[1]
            send_zx(auxzx, zxs.at[ITERS], zxr.at[ITERS])
            fill_teacher(z)
            z_chain(2)
        else:
            wait_for(auxzx.at[pl.ds(0, NP - 1)], zxr.at[ITERS])
            expsum = unpack(jnp.sum(auxzx[...], axis=0), 0, 3)
            lse = jnp.log(expsum)
            weight = rw_ref[...] * 10.0
            alpha = weight / expsum
            abuf[y] = pack([alpha], 4)
            send_y(abuf, abs_.at[0], abr.at[0])
            z_chain(3)
            fill_teacher(z_at(1))
            fill_teacher(z_at(NZ - 1))
        wait_for(ybuf.at[it, pl.ds(0, NY - 1)], yr.at[it])
        colscale = 1.0 / jnp.sum(ybuf[it], axis=0)
        cvec[...] = colscale
        if not last:
            (tot,) = row_sums(lambda b: two_rows(cvec[b : b + 1, :]), [expo])
            zxbuf[it, pr] = pack([tot], 8)
        else:
            tot, qz = row_sums(lambda b: two_rows(cvec[b : b + 1, :]), [expo, expoz])
            c3buf[0] = pack([other(tot), other(qz)], 8)
            send_core(c3buf.at[0], c3buf.at[1], cs.at[it], cr.at[it])
            mine = pack([own(tot), own(qz)], 8)
            wait_for(c3buf.at[1], cr.at[it])
            zxbuf[it, pr] = mine + c3buf[1]
        send_zx(zxbuf.at[it], zxs.at[it], zxr.at[it])
        if it == 0:
            z_chain(1)
            y_chain(2)
            student_z(0)
        elif it == 1:
            y_chain(3)
            fill_student(y_at(1))
            fill_student(y_at(NY - 1))
            student_x(0)
        else:
            sum_protos(1, expo, colscale)
            y_chain(4)
            z_chain(4)
            fill_student(y_at(2))
            fill_student(y_at(NY - 2))
        wait_for(zxbuf.at[it, pl.ds(0, NP - 1)], zxr.at[it])
        sums = jnp.sum(zxbuf[it], axis=0)
        if not last:
            cbuf[it, c] = sums
            send_core(cbuf.at[it, c], cbuf.at[it, c], cs.at[it], cr.at[it])
            wait_for(cbuf.at[it, o], cr.at[it])
            rowscale = 1.0 / unpack(cbuf[it, 0] + cbuf[it, 1], 0, 6)
    rowscale = 1.0 / unpack(sums, 0, 3)
    loss_ref[...] = lse - rowscale * unpack(sums, 3, 3)
    beta = weight * rowscale
    bbuf[y] = pack([beta], 4)
    send_y(bbuf, abs_.at[1], abr.at[1])

    student_z(1)
    fill_teacher(z_at(2))
    fill_teacher(z_at(NZ - 2))
    fill_teacher(z_at(3))
    fill_teacher(z_at(NZ - 3))
    fill_student(y_at(3))
    fill_student(y_at(NY - 3))
    y_chain_end()
    z_chain_end()
    fill_student(y_at(4))
    fill_teacher(z_at(4))
    wait_for(abuf.at[pl.ds(0, NY - 1)], abr.at[0])

    def scale_students(buf):
        for g in range(NY):
            factor = unpack(buf[g], 0, 3)
            scaled[:, g * R : (g + 1) * R] = (snt[g].astype(F32) * factor).astype(BF16)

    scale_students(abuf)

    def student_part(h):
        right = jnp.concatenate([pf[g, h] for g in range(NY)], axis=0)
        return jnp.dot(scaled[...], right, preferred_element_type=F32)

    def teacher_part(h):
        right = ef[h].reshape(NY * R, KB)
        return jnp.dot(scaled[...], right, preferred_element_type=F32)

    vsend[...] = student_part(o).astype(BF16)
    send_core(vsend, vrecv, vbs.at[0], vbr.at[0])
    vacc[...] = student_part(c)
    student_x(1)
    wait_for(bbuf.at[pl.ds(0, NY - 1)], abr.at[1])
    scale_students(bbuf)
    bsend[...] = teacher_part(o).astype(BF16)
    send_core(bsend, brecv, vbs.at[1], vbr.at[1])
    teacher = teacher_part(c)

    rows = lax.broadcasted_iota(jnp.int32, (16, R), 0)
    lanes = lax.broadcasted_iota(jnp.int32, (16, R), 1)
    pick = jnp.where((lanes == rows + pr * PR) & (rows < PR), 1.0, 0.0)
    dsn = jnp.sum(pick * alpha, axis=1, keepdims=True) * student_end(0)
    dsn = dsn - jnp.sum(pick * beta, axis=1, keepdims=True) * student_end(1)
    mine = jnp.dot(pick.astype(BF16), s_ref[...], preferred_element_type=F32)
    inv = lax.rsqrt(jnp.sum(mine * mine, axis=1, keepdims=True) + EPS)
    mine = mine * inv
    grad = (dsn - mine * jnp.sum(mine * dsn, axis=1, keepdims=True)) * inv
    gs_ref[...] = grad[:PR]

    wait_for(vrecv, vbr.at[0])
    wait_for(brecv, vbr.at[1])
    xg = vacc[...] + vrecv[...].astype(F32) - cvec[pl.ds(y, 1), :] * (teacher + brecv[...].astype(F32))
    xg = xg.T
    floats = wraw[y].astype(F32)
    inv = lax.rsqrt(jnp.sum(floats * floats, axis=1, keepdims=True) + EPS)
    unit = floats * inv
    gp_ref[...] = ((xg - unit * jnp.sum(unit * xg, axis=1, keepdims=True)) * inv).astype(BF16)

    for ref, sem in late:
        wait_for(ref, sem)


def shards(teacher_feat, student_feat, prototypes, row_weight):
    vmem = pl.BlockSpec(memory_space=pltpu.VMEM)
    dma = pltpu.SemaphoreType.DMA
    scratch = [
        pltpu.VMEM((NB, KB, D), BF16),
        pltpu.VMEM((2 * KB, D), BF16),
        pltpu.VMEM((NB, KB, D), BF16),
        pltpu.VMEM((NB, D, KB), BF16),
        pltpu.VMEM((NC, KB, D), BF16),
        pltpu.VMEM((NC, R, D), BF16),
        pltpu.VMEM((NC, R, D), BF16),
        pltpu.VMEM((NZ, NY, ZR, D), BF16),
        pltpu.VMEM((NY, R, D), BF16),
        pltpu.VMEM((NY, D, R), BF16),
        pltpu.VMEM((NB, NC, R, KB), BF16),
        pltpu.VMEM((NB, NC, R, KB), BF16),
        pltpu.VMEM((NB, NC, R, KB), BF16),
        pltpu.VMEM((NC, NY, NZ, ZR, KB), BF16),
        pltpu.VMEM((NY, NC, R, KB), BF16),
        pltpu.VMEM((2, NC, R, D), F32),
        pltpu.VMEM((D, KB), F32),
        pltpu.VMEM((D, NY * R), BF16),
        pltpu.VMEM((NB, KB), F32),
        pltpu.VMEM((ITERS, NY, NB, KB), F32),
        pltpu.VMEM((ITERS, NP, 8, 128), F32),
        pltpu.VMEM((ITERS - 1, NC, 8, 128), F32),
        pltpu.VMEM((2, 8, 128), F32),
        pltpu.VMEM((2, 4, 128), F32),
        pltpu.VMEM((NP, 4, 128), F32),
        pltpu.VMEM((NY, 4, 128), F32),
        pltpu.VMEM((NY, 4, 128), F32),
        pltpu.VMEM((2, R, D), BF16),
        pltpu.VMEM((2, R, D), BF16),
        pltpu.VMEM((2, NZ, ZR, D), BF16),
        pltpu.VMEM((2, NZ, ZR, D), BF16),
        pltpu.VMEM((2, NX, 16, D), BF16),
        pltpu.VMEM((2, NX, 16, D), BF16),
        pltpu.VMEM((D, KB), BF16),
        pltpu.VMEM((D, KB), BF16),
        pltpu.VMEM((D, KB), BF16),
        pltpu.VMEM((D, KB), BF16),
        dma((NB + 1,)),
        dma((2,)), dma((2,)),
        dma((ITERS,)), dma((ITERS,)),
        dma((ITERS + 1,)), dma((ITERS + 1,)),
        dma((ITERS + 1,)), dma((ITERS + 1,)),
        dma((1,)), dma((1,)),
        dma((2, 4)), dma((2, 4)),
        dma((2, 4)), dma((2, 4)),
        dma((2,)), dma((2,)),
        dma((2, 3)), dma((2, 3)),
        dma((2,)), dma((2,)),
    ]
    loss, grad_student, grad_proto = pl.pallas_call(
        kernel,
        out_shape=(
            jax.ShapeDtypeStruct((1, R), F32),
            jax.ShapeDtypeStruct((PR, D), F32),
            jax.ShapeDtypeStruct((KB, D), BF16),
        ),
        in_specs=[vmem, vmem, pl.BlockSpec(memory_space=pl.ANY), vmem],
        out_specs=(vmem, vmem, vmem),
        scratch_shapes=scratch,
        compiler_params=pltpu.CompilerParams(
            collective_id=0, has_side_effects=True, vmem_limit_bytes=56 * 2**20
        ),
        name="sinkhorn_head",
    )(teacher_feat, student_feat, prototypes, row_weight.reshape(1, R))
    return (loss.reshape(R), grad_student, grad_proto)


def solution(mesh):
    return jax.shard_map(
        shards,
        mesh=mesh,
        in_specs=(P("dp", None), P("dp", None), P("proto", None), P("dp")),
        out_specs=(P("dp"), P(("dp", "proto"), None), P(("proto", "dp"), None)),
        check_vma=False,
    )
```

time: 527 us -> 103 us (0.20)
  the two profiles are of different devices: /device:TPU:70 before, /device:TPU:1 now
where the time goes in v1:
time: 103 us; the launch traced here: 102 us
  Pallas kernels  96.2 us (93%)
  local copies, waits for them, and re-layouts  4.21 us (4%)
  other arithmetic  1.25 us (1%)
    pallas_call x1, Pallas kernels, shards(): pl.pallas_call(kernel, out_shape=(jax.ShapeDtypeStruct((1, R), F32), jax....  96.2 us
    unnamed x2, local copies, waits for them, and re-layouts  2.97 us

profile of v1, /device:TPU:1, one launch (start us, length us, event | category | flops | bytes accessed | tf_op | source)
XLA Modules:
  0.0 102.3 jit_solution(17678273233838735617)
XLA Ops:
  0.6 1.2 %reshape.12.rw_ref = f32[1,384]{1,0:T(1,128)} reshape(f32[384]{0:T(512)} %param.7) | data formatting | bytes 3072 | tf_op jit(solution)/shard_map/reshape | solution.py:475
  1.9 96.2 %sinkhorn_head.1 = (f32[1,384]{1,0:T(1,128)}, f32[12,384]{1,0:T(8,128)}, bf16[256,384]{1,0:T(8,128)(2,1)}) custom-call(bf16[384,384]{1,0:T(8,128)(2,1)} %t_ref.1, bf16[384,384]{1,0:T(8,128)(2,1)} %s_ref.1, bf16[4096,384]{1,0:T(8,128)(2,1)} %w_ref.1, f32[1,384]{1,0:T(1,128)} %reshape.12.rw_ref), custom_call_target="tpu_custom_call" | custom-call | tf_op jit(solution)/shard_map/sinkhorn_head/pallas_call | solution.py:461
  98.1 1.2 %reduce = f32[384]{0:T(512)} reduce(f32[1,384]{1,0:T(1,128)} %get-tuple-element.6, f32[]{:T(128)} %constant), dimensions={0}, to_apply=%get-tuple-element.6.reduce_sub_computation | reduce | bytes 3076 | tf_op jit(solution)/shard_map/sinkhorn_head/pallas_call | solution.py:461
  99.3 1.3 %copy.9 = f32[12,384]{1,0:T(8,128)} copy(f32[12,384]{1,0:T(8,128)} %get-tuple-element.13) | data formatting | bytes 36864
  100.7 1.6 %copy.10 = bf16[256,384]{1,0:T(8,128)(2,1)} copy(bf16[256,384]{1,0:T(8,128)(2,1)} %get-tuple-element.14) | data formatting | bytes 393216

commit v2 on v1

--- a/solution.py
+++ b/solution.py
@@ -1,3 +1,5 @@
+import math
+
 import jax
 import jax.numpy as jnp
 from jax import lax
@@ -17,6 +19,7 @@
 ZR = R // NZ
 PR = R // NP
 EPS = 1e-6
+EXPO_SCALE = 25.0 * math.log2(math.e)
 NT = (((1,), (1,)), ((), ()))
 
 
@@ -114,49 +117,40 @@
     for peer in peers:
         pl.semaphore_signal(barrier, inc=1, device_id=peer, device_id_type=MESH)
 
-    tn2[c] = unit_rows(t_ref[...]).astype(BF16)
+    tn_own = unit_rows(t_ref[...]).astype(BF16)
+    tn2[c] = tn_own
+
+    def expo_block(b, h):
+        e = jnp.exp2(lax.dot_general(tn2[h], wn[b], NT, preferred_element_type=F32) * EXPO_SCALE)
+        expo[b, h] = e.astype(BF16)
+        return jnp.sum(e, axis=0, keepdims=True)
+
+    for b in range(NB):
+        loads[b].wait()
+        wn[b] = unit_rows(wraw[b]).astype(BF16)
+        ybuf[0, y, b : b + 1, :] = expo_block(b, c)
     sn_own = unit_rows(s_ref[...]).astype(BF16)
     sn2[c] = sn_own
-    gs[y] = sn_own
-    gt[z, y] = tn2[c, pl.ds(pl.multiple_of(z * ZR, 16), ZR), :]
-    for load in loads:
-        load.wait()
-
-    def norm_block(b, carry):
-        block = unit_rows(wraw[b]).astype(BF16)
-        wn[b] = block
-        wnt[b] = block.T
-        return carry
-
-    lax.fori_loop(0, NB, norm_block, 0)
-    for h in range(NC):
-        wnf[h] = unit_rows(wfraw[pl.ds(h * KB, KB), :]).astype(BF16)
-
-    def score_rows(h, first):
-        def block(b, carry):
-            w = wn[b]
-            st = lax.dot_general(tn2[h], w, NT, preferred_element_type=F32)
-            e = jnp.exp(st * 25.0)
-            zs = lax.dot_general(sn2[h], w, NT, preferred_element_type=F32) * 10.0
-            expo[b, h] = e.astype(BF16)
-            expoz[b, h] = (e * zs).astype(BF16)
-            prob[b, h] = jnp.exp(zs).astype(BF16)
-            total = jnp.sum(e, axis=0, keepdims=True)
-            if not first:
-                total = total + ybuf[0, y, pl.ds(b, 1), :]
-            ybuf[0, y, pl.ds(b, 1), :] = total
-            return carry
-
-        lax.fori_loop(0, NB, block, 0)
-
-    score_rows(c, True)
 
     pl.semaphore_wait(barrier, len(peers))
     send_core(tn2.at[c], tn2.at[c], xs.at[0], xr.at[0])
-    send_core(sn2.at[c], sn2.at[c], xs.at[1], xr.at[1])
+    gt[z, y] = tn2[c, pl.ds(pl.multiple_of(z * ZR, 16), ZR), :]
     for a in Y_STEPS:
         send(gt.at[z, y], gt.at[z, y], gts.at[0], gtr.at[0], dev(y_at(a), c, z, x))
     late.append((gt.at[0, pl.ds(0, NY - 1)], gts.at[0]))
+    send_core(sn2.at[c], sn2.at[c], xs.at[1], xr.at[1])
+    gs[y] = sn_own
+
+    def student_block(b, h):
+        zs = lax.dot_general(sn2[h], wn[b], NT, preferred_element_type=F32) * 10.0
+        prob[b, h] = jnp.exp(zs).astype(BF16)
+        expoz[b, h] = (expo[b, h].astype(F32) * zs).astype(BF16)
+
+    for b in range(NB // 2):
+        student_block(b, c)
+    wait_for(tn2.at[o], xr.at[0])
+    for b in range(NB):
+        ybuf[0, y, b : b + 1, :] += expo_block(b, o)
 
     def y_chain(step):
         if step > 1:
@@ -194,7 +188,7 @@
         rows = gt[slice_].reshape(R, D)
         for h in range(NC):
             st = lax.dot_general(rows, wnf[h], NT, preferred_element_type=F32)
-            e = jnp.exp(st * 25.0).astype(BF16)
+            e = jnp.exp2(st * EXPO_SCALE).astype(BF16)
             for g in range(NY):
                 ef[h, g, slice_] = e[g * ZR : (g + 1) * ZR]
 
@@ -204,12 +198,6 @@
         for h in range(NC):
             zs = lax.dot_general(rows, wnf[h], NT, preferred_element_type=F32) * 10.0
             pf[group, h] = jnp.exp(zs).astype(BF16)
-
-    y_chain(1)
-    fill_student(y)
-    wait_for(tn2.at[o], xr.at[0])
-    wait_for(sn2.at[o], xr.at[1])
-    score_rows(o, False)
 
     def own(v):
         return jnp.where(c == 0, v[:, :R], v[:, R:])
@@ -243,29 +231,29 @@
         ucs[q] = uw[q, o].astype(BF16)
         send_core(ucs.at[q], ucr.at[q], us.at[q, 0], ur.at[q, 0])
 
-    def student_z(q):
+    def student_x(q):
         wait_for(ucr.at[q], ur.at[q, 0])
         total = uw[q, c] + ucr[q].astype(F32)
-        uzs[q] = total.astype(BF16).reshape(NZ, ZR, D)
+        pad = jnp.zeros((16 - PR, D), F32)
+        for i in range(NP):
+            tile = jnp.concatenate([total[i * PR : (i + 1) * PR], pad], axis=0)
+            uxs[q, i % NX, i // NX] = tile.astype(BF16)
+        uxr[q, x] = uxs[q, x]
+        for a in X_STEPS:
+            send(uxs.at[q, x_at(a)], uxr.at[q, x], us.at[q, 1], ur.at[q, 1], dev(y, c, z, x_at(a)))
+        late.append((uxs.at[q, pl.ds(0, NX - 1)], us.at[q, 1]))
+
+    def student_z(q):
+        wait_for(uxr.at[q, pl.ds(0, NX - 1)], ur.at[q, 1])
+        uzs[q] = jnp.sum(uxr[q].astype(F32), axis=0).astype(BF16)
         uzr[q, z] = uzs[q, z]
         for a in Z_STEPS:
-            send(uzs.at[q, z_at(a)], uzr.at[q, z], us.at[q, 1], ur.at[q, 1], dev(y, c, z_at(a), x))
-        late.append((uzs.at[q, pl.ds(0, NZ - 1)], us.at[q, 1]))
-
-    def student_x(q):
-        wait_for(uzr.at[q, pl.ds(0, NZ - 1)], ur.at[q, 1])
-        total = jnp.sum(uzr[q].astype(F32), axis=0)
-        pad = jnp.zeros((16 - PR, D), F32)
-        for i in range(NX):
-            uxs[q, i] = jnp.concatenate([total[i * PR : (i + 1) * PR], pad], axis=0).astype(BF16)
-        uxr[q, x] = uxs[q, x]
-        for a in X_STEPS:
-            send(uxs.at[q, x_at(a)], uxr.at[q, x], us.at[q, 2], ur.at[q, 2], dev(y, c, z, x_at(a)))
-        late.append((uxs.at[q, pl.ds(0, NX - 1)], us.at[q, 2]))
+            send(uzs.at[q, z_at(a)], uzr.at[q, z], us.at[q, 2], ur.at[q, 2], dev(y, c, z_at(a), x))
+        late.append((uzs.at[q, pl.ds(0, NZ - 1)], us.at[q, 2]))
 
     def student_end(q):
-        wait_for(uxr.at[q, pl.ds(0, NX - 1)], ur.at[q, 2])
-        return jnp.sum(uxr[q].astype(F32), axis=0)
+        wait_for(uzr.at[q, pl.ds(0, NZ - 1)], ur.at[q, 2])
+        return jnp.sum(uzr[q].astype(F32), axis=0)
 
     rowscale = None
     for it in range(ITERS):
@@ -277,30 +265,36 @@
                 ybuf[it, y, b : b + 1, :] = both[0:1] + both[1:2]
         send_y(ybuf.at[it], ys.at[it], yr.at[it])
         if it == 0:
-            rows16 = lax.broadcasted_iota(jnp.int32, (16, KB), 0)
-            ones = jnp.where(rows16 == 0, 1.0, 0.0).astype(BF16)
-            (expsum,) = row_sums(lambda b: ones, [prob])
-            auxc[0] = pack([other(expsum)], 4)
-            send_core(auxc.at[0], auxc.at[1], cs.at[ITERS], cr.at[ITERS])
-            expsum_own = own(expsum)
-            sum_protos(0, prob, None)
+            y_chain(1)
+            for b in range(NB // 2, NB):
+                student_block(b, c)
+            wait_for(sn2.at[o], xr.at[1])
+            for b in range(NB):
+                student_block(b, o)
+            z_chain(1)
         elif it == 1:
             wait_for(auxc.at[1], cr.at[ITERS])
             auxzx[pr] = pack([expsum_own], 4) + auxc[1]
             send_zx(auxzx, zxs.at[ITERS], zxr.at[ITERS])
-            fill_teacher(z)
+            y_chain(2)
             z_chain(2)
+            fill_student(y_at(1))
+            fill_student(y_at(NY - 1))
         else:
             wait_for(auxzx.at[pl.ds(0, NP - 1)], zxr.at[ITERS])
             expsum = unpack(jnp.sum(auxzx[...], axis=0), 0, 3)
             lse = jnp.log(expsum)
-            weight = rw_ref[...] * 10.0
+            weight = rw_ref[...].reshape(1, R) * 10.0
             alpha = weight / expsum
             abuf[y] = pack([alpha], 4)
             send_y(abuf, abs_.at[0], abr.at[0])
-            z_chain(3)
-            fill_teacher(z_at(1))
-            fill_teacher(z_at(NZ - 1))
+            student_z(0)
+            fill_student(y_at(2))
+            fill_student(y_at(NY - 2))
+            fill_teacher(z_at(2))
+            fill_teacher(z_at(NZ - 2))
+            y_chain(4)
+            z_chain(4)
         wait_for(ybuf.at[it, pl.ds(0, NY - 1)], yr.at[it])
         colscale = 1.0 / jnp.sum(ybuf[it], axis=0)
         cvec[...] = colscale
@@ -316,20 +310,33 @@
             zxbuf[it, pr] = mine + c3buf[1]
         send_zx(zxbuf.at[it], zxs.at[it], zxr.at[it])
         if it == 0:
-            z_chain(1)
-            y_chain(2)
-            student_z(0)
+            rows16 = lax.broadcasted_iota(jnp.int32, (16, KB), 0)
+            ones = jnp.where(rows16 == 0, 1.0, 0.0).astype(BF16)
+            (expsum,) = row_sums(lambda b: ones, [prob])
+            auxc[0] = pack([other(expsum)], 4)
+            send_core(auxc.at[0], auxc.at[1], cs.at[ITERS], cr.at[ITERS])
+            expsum_own = own(expsum)
+            for b in range(NB):
+                wnt[b] = wn[b].T
+            sum_protos(0, prob, None)
+            loads[NB].wait()
+            for h in range(NC):
+                wnf[h] = unit_rows(wfraw[pl.ds(h * KB, KB), :]).astype(BF16)
+            fill_student(y)
         elif it == 1:
+            fill_teacher(z)
+            fill_teacher(z_at(1))
+            fill_teacher(z_at(NZ - 1))
+            student_x(0)
             y_chain(3)
-            fill_student(y_at(1))
-            fill_student(y_at(NY - 1))
-            student_x(0)
+            z_chain(3)
         else:
             sum_protos(1, expo, colscale)
-            y_chain(4)
-            z_chain(4)
-            fill_student(y_at(2))
-            fill_student(y_at(NY - 2))
+            fill_student(y_at(3))
+            fill_student(y_at(NY - 3))
+            fill_teacher(z_at(3))
+            fill_teacher(z_at(NZ - 3))
+            student_x(1)
         wait_for(zxbuf.at[it, pl.ds(0, NP - 1)], zxr.at[it])
         sums = jnp.sum(zxbuf[it], axis=0)
         if not last:
@@ -338,18 +345,11 @@
             wait_for(cbuf.at[it, o], cr.at[it])
             rowscale = 1.0 / unpack(cbuf[it, 0] + cbuf[it, 1], 0, 6)
     rowscale = 1.0 / unpack(sums, 0, 3)
-    loss_ref[...] = lse - rowscale * unpack(sums, 3, 3)
+    loss_ref[...] = (lse - rowscale * unpack(sums, 3, 3)).reshape(R)
     beta = weight * rowscale
     bbuf[y] = pack([beta], 4)
     send_y(bbuf, abs_.at[1], abr.at[1])
 
-    student_z(1)
-    fill_teacher(z_at(2))
-    fill_teacher(z_at(NZ - 2))
-    fill_teacher(z_at(3))
-    fill_teacher(z_at(NZ - 3))
-    fill_student(y_at(3))
-    fill_student(y_at(NY - 3))
     y_chain_end()
     z_chain_end()
     fill_student(y_at(4))
@@ -374,12 +374,21 @@
     vsend[...] = student_part(o).astype(BF16)
     send_core(vsend, vrecv, vbs.at[0], vbr.at[0])
     vacc[...] = student_part(c)
-    student_x(1)
     wait_for(bbuf.at[pl.ds(0, NY - 1)], abr.at[1])
     scale_students(bbuf)
     bsend[...] = teacher_part(o).astype(BF16)
     send_core(bsend, brecv, vbs.at[1], vbr.at[1])
+    student_z(1)
     teacher = teacher_part(c)
+
+    wait_for(vrecv, vbr.at[0])
+    wait_for(brecv, vbr.at[1])
+    xg = vacc[...] + vrecv[...].astype(F32) - cvec[pl.ds(y, 1), :] * (teacher + brecv[...].astype(F32))
+    xg = xg.T
+    floats = wraw[y].astype(F32)
+    inv = lax.rsqrt(jnp.sum(floats * floats, axis=1, keepdims=True) + EPS)
+    unit = floats * inv
+    gp_ref[...] = ((xg - unit * jnp.sum(unit * xg, axis=1, keepdims=True)) * inv).astype(BF16)
 
     rows = lax.broadcasted_iota(jnp.int32, (16, R), 0)
     lanes = lax.broadcasted_iota(jnp.int32, (16, R), 1)
@@ -392,21 +401,19 @@
     grad = (dsn - mine * jnp.sum(mine * dsn, axis=1, keepdims=True)) * inv
     gs_ref[...] = grad[:PR]
 
-    wait_for(vrecv, vbr.at[0])
-    wait_for(brecv, vbr.at[1])
-    xg = vacc[...] + vrecv[...].astype(F32) - cvec[pl.ds(y, 1), :] * (teacher + brecv[...].astype(F32))
-    xg = xg.T
-    floats = wraw[y].astype(F32)
-    inv = lax.rsqrt(jnp.sum(floats * floats, axis=1, keepdims=True) + EPS)
-    unit = floats * inv
-    gp_ref[...] = ((xg - unit * jnp.sum(unit * xg, axis=1, keepdims=True)) * inv).astype(BF16)
-
     for ref, sem in late:
         wait_for(ref, sem)
 
 
+def write_outputs(loss_in, gs_in, gp_in, loss_ref, gs_ref, gp_ref):
+    loss_ref[...] = loss_in[...]
+    gs_ref[...] = gs_in[...]
+    gp_ref[...] = gp_in[...]
+
+
 def shards(teacher_feat, student_feat, prototypes, row_weight):
     vmem = pl.BlockSpec(memory_space=pltpu.VMEM)
+    anywhere = pl.BlockSpec(memory_space=pl.ANY)
     dma = pltpu.SemaphoreType.DMA
     scratch = [
         pltpu.VMEM((NB, KB, D), BF16),
@@ -438,10 +445,10 @@
         pltpu.VMEM((NY, 4, 128), F32),
         pltpu.VMEM((2, R, D), BF16),
         pltpu.VMEM((2, R, D), BF16),
-        pltpu.VMEM((2, NZ, ZR, D), BF16),
-        pltpu.VMEM((2, NZ, ZR, D), BF16),
-        pltpu.VMEM((2, NX, 16, D), BF16),
-        pltpu.VMEM((2, NX, 16, D), BF16),
+        pltpu.VMEM((2, NZ, 16, D), BF16),
+        pltpu.VMEM((2, NZ, 16, D), BF16),
+        pltpu.VMEM((2, NX, NZ, 16, D), BF16),
+        pltpu.VMEM((2, NX, NZ, 16, D), BF16),
         pltpu.VMEM((D, KB), BF16),
         pltpu.VMEM((D, KB), BF16),
         pltpu.VMEM((D, KB), BF16),
@@ -461,19 +468,29 @@
     loss, grad_student, grad_proto = pl.pallas_call(
         kernel,
         out_shape=(
-            jax.ShapeDtypeStruct((1, R), F32),
+            jax.ShapeDtypeStruct((R,), F32),
             jax.ShapeDtypeStruct((PR, D), F32),
             jax.ShapeDtypeStruct((KB, D), BF16),
         ),
-        in_specs=[vmem, vmem, pl.BlockSpec(memory_space=pl.ANY), vmem],
+        in_specs=[vmem, vmem, anywhere, vmem],
         out_specs=(vmem, vmem, vmem),
         scratch_shapes=scratch,
         compiler_params=pltpu.CompilerParams(
             collective_id=0, has_side_effects=True, vmem_limit_bytes=56 * 2**20
         ),
         name="sinkhorn_head",
-    )(teacher_feat, student_feat, prototypes, row_weight.reshape(1, R))
-    return (loss.reshape(R), grad_student, grad_proto)
+    )(teacher_feat, student_feat, prototypes, row_weight)
+    return pl.pallas_call(
+        write_outputs,
+        out_shape=(
+            jax.ShapeDtypeStruct((R,), F32),
+            jax.ShapeDtypeStruct((PR, D), F32),
+            jax.ShapeDtypeStruct((KB, D), BF16),
+        ),
+        in_specs=[vmem] * 3,
+        out_specs=(vmem,) * 3,
+        name="write_outputs",
+    )(loss, grad_student, grad_proto)
 
 
 def solution(mesh):

time: 103 us -> 85.4 us (0.83)
  Pallas kernels: 96.2 us -> 84.2 us
  local copies, waits for them, and re-layouts: 4.21 us -> 0 us
  other arithmetic: 1.25 us -> 0 us
    pallas_call x1 -> x2, Pallas kernels: 96.2 us -> 84.2 us  [the longest x1 82.5 us: shards(): pl.pallas_call(kernel, out_shape=(jax.ShapeDtypeStruct((R,), F32), jax.Sh...]
    unnamed x2 -> x0, local copies, waits for them, and re-layouts: 2.97 us -> none
    pallas_call x1 -> x0, other arithmetic: 1.25 us -> none  [shards(): pl.pallas_call(kernel, out_shape=(jax.ShapeDtypeStruct((1, R), F32), jax....]
    reshape x1 -> x0, local copies, waits for them, and re-layouts: 1.25 us -> none  [shards(): row_weight.reshape(1, R)]
where the time goes in v2:
time: 85.4 us; the launch traced here: 84.8 us
  Pallas kernels  84.2 us (99%)
    pallas_call x1, Pallas kernels, shards(): pl.pallas_call(kernel, out_shape=(jax.ShapeDtypeStruct((R,), F32), jax.Sh...  82.5 us

profile of v2, /device:TPU:1, one launch (start us, length us, event | category | flops | bytes accessed | tf_op | source)
XLA Modules:
  0.0 84.8 jit_solution(14553625773463619543)
XLA Ops:
  0.6 82.5 %sinkhorn_head.1 = (f32[384]{0:T(512)}, f32[12,384]{1,0:T(8,128)}, bf16[256,384]{1,0:T(8,128)(2,1)}) custom-call(bf16[384,384]{1,0:T(8,128)(2,1)} %t_ref.1, bf16[384,384]{1,0:T(8,128)(2,1)} %s_ref.1, bf16[4096,384]{1,0:T(8,128)(2,1)} %w_ref.1, f32[384]{0:T(512)} %rw_ref.1), custom_call_target="tpu_custom_call" | custom-call | tf_op jit(solution)/shard_map/sinkhorn_head/pallas_call | solution.py:468
  83.1 1.6 %write_outputs.1 = (f32[384]{0:T(512)}, f32[12,384]{1,0:T(8,128)}, bf16[256,384]{1,0:T(8,128)(2,1)}) custom-call(f32[384]{0:T(512)} %get-tuple-element.6.loss_in, f32[12,384]{1,0:T(8,128)} %get-tuple-element.7.gs_in, bf16[256,384]{1,0:T(8,128)(2,1)} %get-tuple-element.8.gp_in), custom_call_target="tpu_custom_call" | custom-call | tf_op jit(solution)/shard_map/write_outputs/pallas_call | solution.py:483

commit v3 on v2

--- a/solution.py
+++ b/solution.py
@@ -16,7 +16,8 @@
 D = 384
 KB = 256
 NB = 8
-ZR = R // NZ
+PIECE = 32
+PIECES = R // PIECE
 PR = R // NP
 EPS = 1e-6
 EXPO_SCALE = 25.0 * math.log2(math.e)
@@ -64,7 +65,7 @@
     wraw, wfraw, wn, wnt, wnf, tn2, sn2, gt, gs, snt, expo, expoz, prob, ef, pf, uw,
     vacc, scaled, cvec, ybuf, zxbuf, cbuf, c3buf, auxc, auxzx, abuf, bbuf,
     ucs, ucr, uzs, uzr, uxs, uxr, vsend, vrecv, bsend, brecv,
-    wsem, xs, xr, ys, yr, zxs, zxr, cs, cr, gts, gtr, tcs, tcr, scs, scr, abs_, abr,
+    wsem, xs, xr, ys, yr, zxs, zxr, cs, cr, gts, gtr, tcs, tcr, hcs, hcr, scs, scr, abs_, abr,
     us, ur, vbs, vbr,
 ):
     dp, pr = lax.axis_index("dp"), lax.axis_index("proto")
@@ -131,26 +132,11 @@
         ybuf[0, y, b : b + 1, :] = expo_block(b, c)
     sn_own = unit_rows(s_ref[...]).astype(BF16)
     sn2[c] = sn_own
-
-    pl.semaphore_wait(barrier, len(peers))
-    send_core(tn2.at[c], tn2.at[c], xs.at[0], xr.at[0])
-    gt[z, y] = tn2[c, pl.ds(pl.multiple_of(z * ZR, 16), ZR), :]
-    for a in Y_STEPS:
-        send(gt.at[z, y], gt.at[z, y], gts.at[0], gtr.at[0], dev(y_at(a), c, z, x))
-    late.append((gt.at[0, pl.ds(0, NY - 1)], gts.at[0]))
-    send_core(sn2.at[c], sn2.at[c], xs.at[1], xr.at[1])
-    gs[y] = sn_own
-
-    def student_block(b, h):
-        zs = lax.dot_general(sn2[h], wn[b], NT, preferred_element_type=F32) * 10.0
-        prob[b, h] = jnp.exp(zs).astype(BF16)
-        expoz[b, h] = (expo[b, h].astype(F32) * zs).astype(BF16)
-
-    for b in range(NB // 2):
-        student_block(b, c)
-    wait_for(tn2.at[o], xr.at[0])
     for b in range(NB):
-        ybuf[0, y, b : b + 1, :] += expo_block(b, o)
+        wnt[b] = wn[b].T
+    loads[NB].wait()
+    for h in range(NC):
+        wnf[h] = unit_rows(wfraw[pl.ds(h * KB, KB), :]).astype(BF16)
 
     def y_chain(step):
         if step > 1:
@@ -184,13 +170,53 @@
         for way in range(2):
             wait_for(gt.at[z_at(4), pl.ds(way * (NY // 2), NY // 2)], tcr.at[way, 3])
 
-    def fill_teacher(slice_):
-        rows = gt[slice_].reshape(R, D)
+    def x_chain(step):
+        if step == 1:
+            wait_for(gt.at[NZ + x, pl.ds(0, NY - 1)], gtr.at[1])
+        else:
+            for way, back in ((0, -1), (1, 1)):
+                wait_for(gt.at[NZ + x_at(NX + back)], hcr.at[way, 0])
+        for way, back, to in ((0, -(step - 1), 1), (1, step - 1, -1)):
+            src = gt.at[NZ + x_at(NX + back)]
+            if step == 2:
+                src = src.at[pl.ds(way * (NY // 2), NY // 2)]
+            send(src, src, hcs.at[way, step - 1], hcr.at[way, step - 1], dev(y, c, z, x_at(NX + to)))
+            late.append((src, hcs.at[way, step - 1]))
+
+    def x_chain_end():
+        for way in range(2):
+            wait_for(gt.at[NZ + x_at(2), pl.ds(way * (NY // 2), NY // 2)], hcr.at[way, 1])
+
+    pl.semaphore_wait(barrier, len(peers))
+    send_core(tn2.at[c], tn2.at[c], xs.at[0], xr.at[0])
+    gs[y] = sn_own
+    send_core(sn2.at[c], sn2.at[c], xs.at[1], xr.at[1])
+
+    def spread_teacher(i):
+        piece = (z, NZ + x)[i]
+        gt[piece, y] = tn2[c, pl.ds(pl.multiple_of(piece * PIECE, PIECE), PIECE), :]
+        for a in Y_STEPS:
+            send(gt.at[piece, y], gt.at[piece, y], gts.at[i], gtr.at[i], dev(y_at(a), c, z, x))
+        late.append((gt.at[0, pl.ds(0, NY - 1)], gts.at[i]))
+
+    def student_block(b, h):
+        zs = lax.dot_general(sn2[h], wn[b], NT, preferred_element_type=F32) * 10.0
+        prob[b, h] = jnp.exp(zs).astype(BF16)
+        expoz[b, h] = (expo[b, h].astype(F32) * zs).astype(BF16)
+
+    for b in range(NB // 2):
+        student_block(b, c)
+    wait_for(tn2.at[o], xr.at[0])
+    for b in range(NB):
+        ybuf[0, y, b : b + 1, :] += expo_block(b, o)
+
+    def fill_teacher(piece):
+        rows = gt[piece].reshape(NY * PIECE, D)
         for h in range(NC):
             st = lax.dot_general(rows, wnf[h], NT, preferred_element_type=F32)
             e = jnp.exp2(st * EXPO_SCALE).astype(BF16)
             for g in range(NY):
-                ef[h, g, slice_] = e[g * ZR : (g + 1) * ZR]
+                ef[h, g, piece] = e[g * PIECE : (g + 1) * PIECE]
 
     def fill_student(group):
         rows = gs[group]
@@ -205,15 +231,22 @@
     def other(v):
         return jnp.where(c == 0, v[:, R:], v[:, :R])
 
-    def row_sums(lhs, mats):
-        sums = [jnp.zeros((16, NC * R), F32) for _ in mats]
+    def row_sums(mat, scale, matmuls):
+        total = jnp.zeros((16, NC * R), F32)
+        lanes = jnp.zeros((NC * R, 128), F32)
         for b in range(NB):
-            left = lhs(b)
-            for i, mat in enumerate(mats):
-                sums[i] = sums[i] + lax.dot_general(
-                    left, mat[b].reshape(NC * R, KB), NT, preferred_element_type=F32
+            block = mat[b].reshape(NC * R, KB)
+            if b < matmuls:
+                total = total + lax.dot_general(
+                    two_rows(scale[b : b + 1, :]), block, NT, preferred_element_type=F32
                 )
-        return [s[0:1] + s[1:2] for s in sums]
+            else:
+                block = block.astype(F32)
+                if scale is not None:
+                    block = block * scale[b : b + 1, :]
+                lanes = lanes + (block[:, :128] + block[:, 128:])
+        vector = jnp.sum(lanes.T, axis=0, keepdims=True)
+        return vector + total[0:1] + total[1:2] if matmuls else vector
 
     def sum_protos(q, mat, scale):
         def half(h, carry):
@@ -265,19 +298,17 @@
                 ybuf[it, y, b : b + 1, :] = both[0:1] + both[1:2]
         send_y(ybuf.at[it], ys.at[it], yr.at[it])
         if it == 0:
-            y_chain(1)
             for b in range(NB // 2, NB):
                 student_block(b, c)
             wait_for(sn2.at[o], xr.at[1])
             for b in range(NB):
                 student_block(b, o)
-            z_chain(1)
         elif it == 1:
             wait_for(auxc.at[1], cr.at[ITERS])
             auxzx[pr] = pack([expsum_own], 4) + auxc[1]
             send_zx(auxzx, zxs.at[ITERS], zxr.at[ITERS])
+            fill_teacher(z)
             y_chain(2)
-            z_chain(2)
             fill_student(y_at(1))
             fill_student(y_at(NY - 1))
         else:
@@ -289,20 +320,28 @@
             abuf[y] = pack([alpha], 4)
             send_y(abuf, abs_.at[0], abr.at[0])
             student_z(0)
-            fill_student(y_at(2))
-            fill_student(y_at(NY - 2))
             fill_teacher(z_at(2))
             fill_teacher(z_at(NZ - 2))
+            fill_teacher(NZ + x)
+        wait_for(ybuf.at[it, pl.ds(0, NY - 1)], yr.at[it])
+        if it == 0:
+            spread_teacher(0)
+            y_chain(1)
+        elif it == 1:
+            z_chain(2)
+            spread_teacher(1)
+        else:
             y_chain(4)
             z_chain(4)
-        wait_for(ybuf.at[it, pl.ds(0, NY - 1)], yr.at[it])
+            x_chain(2)
         colscale = 1.0 / jnp.sum(ybuf[it], axis=0)
         cvec[...] = colscale
         if not last:
-            (tot,) = row_sums(lambda b: two_rows(cvec[b : b + 1, :]), [expo])
+            tot = row_sums(expo, colscale, 3)
             zxbuf[it, pr] = pack([tot], 8)
         else:
-            tot, qz = row_sums(lambda b: two_rows(cvec[b : b + 1, :]), [expo, expoz])
+            tot = row_sums(expo, colscale, 3)
+            qz = row_sums(expoz, colscale, 3)
             c3buf[0] = pack([other(tot), other(qz)], 8)
             send_core(c3buf.at[0], c3buf.at[1], cs.at[it], cr.at[it])
             mine = pack([own(tot), own(qz)], 8)
@@ -310,38 +349,36 @@
             zxbuf[it, pr] = mine + c3buf[1]
         send_zx(zxbuf.at[it], zxs.at[it], zxr.at[it])
         if it == 0:
-            rows16 = lax.broadcasted_iota(jnp.int32, (16, KB), 0)
-            ones = jnp.where(rows16 == 0, 1.0, 0.0).astype(BF16)
-            (expsum,) = row_sums(lambda b: ones, [prob])
+            expsum = row_sums(prob, None, 0)
             auxc[0] = pack([other(expsum)], 4)
             send_core(auxc.at[0], auxc.at[1], cs.at[ITERS], cr.at[ITERS])
             expsum_own = own(expsum)
-            for b in range(NB):
-                wnt[b] = wn[b].T
             sum_protos(0, prob, None)
-            loads[NB].wait()
-            for h in range(NC):
-                wnf[h] = unit_rows(wfraw[pl.ds(h * KB, KB), :]).astype(BF16)
             fill_student(y)
         elif it == 1:
-            fill_teacher(z)
+            student_x(0)
             fill_teacher(z_at(1))
             fill_teacher(z_at(NZ - 1))
-            student_x(0)
             y_chain(3)
-            z_chain(3)
+            fill_student(y_at(2))
+            fill_student(y_at(NY - 2))
         else:
             sum_protos(1, expo, colscale)
             fill_student(y_at(3))
             fill_student(y_at(NY - 3))
+            student_x(1)
             fill_teacher(z_at(3))
             fill_teacher(z_at(NZ - 3))
-            student_x(1)
         wait_for(zxbuf.at[it, pl.ds(0, NP - 1)], zxr.at[it])
         sums = jnp.sum(zxbuf[it], axis=0)
         if not last:
             cbuf[it, c] = sums
             send_core(cbuf.at[it, c], cbuf.at[it, c], cs.at[it], cr.at[it])
+            if it == 0:
+                z_chain(1)
+            else:
+                z_chain(3)
+                x_chain(1)
             wait_for(cbuf.at[it, o], cr.at[it])
             rowscale = 1.0 / unpack(cbuf[it, 0] + cbuf[it, 1], 0, 6)
     rowscale = 1.0 / unpack(sums, 0, 3)
@@ -351,9 +388,7 @@
     send_y(bbuf, abs_.at[1], abr.at[1])
 
     y_chain_end()
-    z_chain_end()
     fill_student(y_at(4))
-    fill_teacher(z_at(4))
     wait_for(abuf.at[pl.ds(0, NY - 1)], abr.at[0])
 
     def scale_students(buf):
@@ -373,6 +408,12 @@
 
     vsend[...] = student_part(o).astype(BF16)
     send_core(vsend, vrecv, vbs.at[0], vbr.at[0])
+    z_chain_end()
+    fill_teacher(z_at(4))
+    x_chain_end()
+    fill_teacher(NZ + x_at(1))
+    fill_teacher(NZ + x_at(NX - 1))
+    fill_teacher(NZ + x_at(2))
     vacc[...] = student_part(c)
     wait_for(bbuf.at[pl.ds(0, NY - 1)], abr.at[1])
     scale_students(bbuf)
@@ -423,13 +464,13 @@
         pltpu.VMEM((NC, KB, D), BF16),
         pltpu.VMEM((NC, R, D), BF16),
         pltpu.VMEM((NC, R, D), BF16),
-        pltpu.VMEM((NZ, NY, ZR, D), BF16),
+        pltpu.VMEM((PIECES, NY, PIECE, D), BF16),
         pltpu.VMEM((NY, R, D), BF16),
         pltpu.VMEM((NY, D, R), BF16),
         pltpu.VMEM((NB, NC, R, KB), BF16),
         pltpu.VMEM((NB, NC, R, KB), BF16),
         pltpu.VMEM((NB, NC, R, KB), BF16),
-        pltpu.VMEM((NC, NY, NZ, ZR, KB), BF16),
+        pltpu.VMEM((NC, NY, PIECES, PIECE, KB), BF16),
         pltpu.VMEM((NY, NC, R, KB), BF16),
         pltpu.VMEM((2, NC, R, D), F32),
         pltpu.VMEM((D, KB), F32),
@@ -458,8 +499,9 @@
         dma((ITERS,)), dma((ITERS,)),
         dma((ITERS + 1,)), dma((ITERS + 1,)),
         dma((ITERS + 1,)), dma((ITERS + 1,)),
-        dma((1,)), dma((1,)),
+        dma((2,)), dma((2,)),
         dma((2, 4)), dma((2, 4)),
+        dma((2, 2)), dma((2, 2)),
         dma((2, 4)), dma((2, 4)),
         dma((2,)), dma((2,)),
         dma((2, 3)), dma((2, 3)),

time: 85.4 us -> 82.4 us (0.965)
  Pallas kernels: 84.2 us -> 81.5 us
    pallas_call x1, Pallas kernels: 82.5 us -> 79.9 us  [shards(): pl.pallas_call(kernel, out_shape=(jax.ShapeDtypeStruct((R,), F32), jax.Sh...]
where the time goes in v3:
time: 82.4 us; the launch traced here: 82.2 us
  Pallas kernels  81.5 us (99%)
    pallas_call x1, Pallas kernels, shards(): pl.pallas_call(kernel, out_shape=(jax.ShapeDtypeStruct((R,), F32), jax.Sh...  79.9 us
    pallas_call x1, Pallas kernels, shards(): pl.pallas_call(write_outputs, out_shape=(jax.ShapeDtypeStruct((R,), F32),...  1.65 us

profile of v3, /device:TPU:1, one launch (start us, length us, event | category | flops | bytes accessed | tf_op | source)
XLA Modules:
  0.0 82.2 jit_solution(6052034193419684991)
XLA Ops:
  0.6 79.9 %sinkhorn_head.1 = (f32[384]{0:T(512)}, f32[12,384]{1,0:T(8,128)}, bf16[256,384]{1,0:T(8,128)(2,1)}) custom-call(bf16[384,384]{1,0:T(8,128)(2,1)} %t_ref.1, bf16[384,384]{1,0:T(8,128)(2,1)} %s_ref.1, bf16[4096,384]{1,0:T(8,128)(2,1)} %w_ref.1, f32[384]{0:T(512)} %rw_ref.1), custom_call_target="tpu_custom_call" | custom-call | tf_op jit(solution)/shard_map/sinkhorn_head/pallas_call | solution.py:510
  80.5 1.6 %write_outputs.1 = (f32[384]{0:T(512)}, f32[12,384]{1,0:T(8,128)}, bf16[256,384]{1,0:T(8,128)(2,1)}) custom-call(f32[384]{0:T(512)} %get-tuple-element.6.loss_in, f32[12,384]{1,0:T(8,128)} %get-tuple-element.7.gs_in, bf16[256,384]{1,0:T(8,128)(2,1)} %get-tuple-element.8.gp_in), custom_call_target="tpu_custom_call" | custom-call | tf_op jit(solution)/shard_map/write_outputs/pallas_call | solution.py:525

commit v4 on v3

--- a/solution.py
+++ b/solution.py
@@ -191,6 +191,7 @@
     send_core(tn2.at[c], tn2.at[c], xs.at[0], xr.at[0])
     gs[y] = sn_own
     send_core(sn2.at[c], sn2.at[c], xs.at[1], xr.at[1])
+    y_chain(1)
 
     def spread_teacher(i):
         piece = (z, NZ + x)[i]
@@ -304,11 +305,11 @@
             for b in range(NB):
                 student_block(b, o)
         elif it == 1:
+            z_chain(2)
             wait_for(auxc.at[1], cr.at[ITERS])
             auxzx[pr] = pack([expsum_own], 4) + auxc[1]
             send_zx(auxzx, zxs.at[ITERS], zxr.at[ITERS])
             fill_teacher(z)
-            y_chain(2)
             fill_student(y_at(1))
             fill_student(y_at(NY - 1))
         else:
@@ -320,18 +321,17 @@
             abuf[y] = pack([alpha], 4)
             send_y(abuf, abs_.at[0], abr.at[0])
             student_z(0)
+            fill_student(y_at(2))
+            fill_student(y_at(NY - 2))
             fill_teacher(z_at(2))
             fill_teacher(z_at(NZ - 2))
             fill_teacher(NZ + x)
         wait_for(ybuf.at[it, pl.ds(0, NY - 1)], yr.at[it])
-        if it == 0:
-            spread_teacher(0)
-            y_chain(1)
-        elif it == 1:
-            z_chain(2)
-            spread_teacher(1)
-        else:
-            y_chain(4)
+        if it < 2:
+            spread_teacher(it)
+        if it > 0:
+            y_chain(it + 2)
+        if last:
             z_chain(4)
             x_chain(2)
         colscale = 1.0 / jnp.sum(ybuf[it], axis=0)
@@ -353,15 +353,14 @@
             auxc[0] = pack([other(expsum)], 4)
             send_core(auxc.at[0], auxc.at[1], cs.at[ITERS], cr.at[ITERS])
             expsum_own = own(expsum)
+            y_chain(2)
             sum_protos(0, prob, None)
             fill_student(y)
+            z_chain(1)
         elif it == 1:
             student_x(0)
             fill_teacher(z_at(1))
             fill_teacher(z_at(NZ - 1))
-            y_chain(3)
-            fill_student(y_at(2))
-            fill_student(y_at(NY - 2))
         else:
             sum_protos(1, expo, colscale)
             fill_student(y_at(3))
@@ -374,9 +373,7 @@
         if not last:
             cbuf[it, c] = sums
             send_core(cbuf.at[it, c], cbuf.at[it, c], cs.at[it], cr.at[it])
-            if it == 0:
-                z_chain(1)
-            else:
+            if it == 1:
                 z_chain(3)
                 x_chain(1)
             wait_for(cbuf.at[it, o], cr.at[it])

time: 82.4 us -> 79.7 us (0.967)
  Pallas kernels: 81.5 us -> 78.7 us
    pallas_call x1, Pallas kernels: 79.9 us -> 77.1 us  [shards(): pl.pallas_call(kernel, out_shape=(jax.ShapeDtypeStruct((R,), F32), jax.Sh...]
where the time goes in v4:
time: 79.7 us; the launch traced here: 79.3 us
  Pallas kernels  78.7 us (99%)
    pallas_call x1, Pallas kernels, shards(): pl.pallas_call(kernel, out_shape=(jax.ShapeDtypeStruct((R,), F32), jax.Sh...  77.1 us
    pallas_call x1, Pallas kernels, shards(): pl.pallas_call(write_outputs, out_shape=(jax.ShapeDtypeStruct((R,), F32),...  1.65 us

profile of v4, /device:TPU:1, one launch (start us, length us, event | category | flops | bytes accessed | tf_op | source)
XLA Modules:
  0.0 79.3 jit_solution(6763815756643791454)
XLA Ops:
  0.6 77.1 %sinkhorn_head.1 = (f32[384]{0:T(512)}, f32[12,384]{1,0:T(8,128)}, bf16[256,384]{1,0:T(8,128)(2,1)}) custom-call(bf16[384,384]{1,0:T(8,128)(2,1)} %t_ref.1, bf16[384,384]{1,0:T(8,128)(2,1)} %s_ref.1, bf16[4096,384]{1,0:T(8,128)(2,1)} %w_ref.1, f32[384]{0:T(512)} %rw_ref.1), custom_call_target="tpu_custom_call" | custom-call | tf_op jit(solution)/shard_map/sinkhorn_head/pallas_call | solution.py:507
  77.7 1.6 %write_outputs.1 = (f32[384]{0:T(512)}, f32[12,384]{1,0:T(8,128)}, bf16[256,384]{1,0:T(8,128)(2,1)}) custom-call(f32[384]{0:T(512)} %get-tuple-element.6.loss_in, f32[12,384]{1,0:T(8,128)} %get-tuple-element.7.gs_in, bf16[256,384]{1,0:T(8,128)(2,1)} %get-tuple-element.8.gp_in), custom_call_target="tpu_custom_call" | custom-call | tf_op jit(solution)/shard_map/write_outputs/pallas_call | solution.py:522
